TPU v7x, 256 devices: a whole 4x4x8 slice. The times are simulated.
256 devices in a mesh: seq: 32 (over y_lo, z, core), head: 8 (over x, y_hi).
Axes of the slice: x: 4, y: 4 (y_hi: 2, y_lo: 2; y = y_hi * 2 + y_lo), z: 8, core: 2. Of those that a mesh axis runs over, the one named last changes fastest.
Arguments:
- queries: bfloat16 [4096, 128, 576], P('seq', 'head'), may hold values from -48 to 48
- latent_cache: bfloat16 [4096, 576], P('seq'), may hold values from -4 to 4
- grad_out: bfloat16 [4096, 128, 512], P('seq', 'head'), may hold values from -6 to 6
- segment_ids: int32 [4096], replicated, may hold values from 0 to 31, never falling along the last dimension, each value on 1 to 256 neighbouring positions
Outputs:
- grad_queries: bfloat16 [4096, 128, 576], P('seq', 'head')
- grad_cache: bfloat16 [4096, 576], P('seq')
Inputs may be any that keep to these rules, and one draw needn't show every extreme that they name: `segment_ids`: document numbers never fall along the sequence; no document has more than 256 tokens and one has exactly 256.
All inputs are finite; a program needn't handle non-finite values.
Results may differ from a plain program's by a relative error of at most 0.0057.
Values may be sent and summed in bfloat16 or wider, within the bound.
A program may use at most 64 MiB of HBM per device.

v0:
```python
import jax
import jax.numpy as jnp
from jax import lax
from jax.sharding import PartitionSpec as P

LATENT = 512
HOPS = 2


score_scale = 192.0 ** (-0.5)
masked_score = -1e30


def shifted(block, axis, distance):
    devices = range(lax.axis_size(axis))
    route = [(i - distance, i) for i in devices if i - distance in devices]
    return lax.ppermute(block, axis, route)


def window_mask(segment_ids, block_index, block_rows, window_rows):
    filler = jnp.full((HOPS * block_rows,), -1, jnp.int32)
    padded = jnp.concatenate([filler, segment_ids])
    offset = block_index * block_rows
    query_seg = lax.dynamic_slice_in_dim(segment_ids, offset, block_rows)
    key_seg = lax.dynamic_slice_in_dim(padded, offset, window_rows)
    query_pos = lax.iota(jnp.int32, block_rows)[:, None] + HOPS * block_rows
    key_pos = lax.iota(jnp.int32, window_rows)[None, :]
    return (query_seg[:, None] == key_seg[None, :]) & (key_pos <= query_pos)


def attend(queries, window, grad_out, visible):
    values = window[:, :LATENT]
    scores = (
        jnp.einsum("ihc,tc->hit", queries, window, preferred_element_type=jnp.float32) * score_scale
    )
    scores = jnp.where(visible[None], scores, masked_score)
    row_max = jnp.max(scores, axis=2, keepdims=True)
    expo_terms = jnp.where(visible[None], jnp.exp(scores - row_max), 0.0)
    weights = expo_terms / jnp.sum(expo_terms, axis=2, keepdims=True)
    weights_low = weights.astype(jnp.bfloat16)
    output = jnp.einsum("hit,tc->ihc", weights_low, values, preferred_element_type=jnp.float32)
    row_delta = jnp.sum(grad_out.astype(jnp.float32) * output, axis=2)
    grad_weights = jnp.einsum("ihc,tc->hit", grad_out, values, preferred_element_type=jnp.float32)
    grad_scores = (
        score_scale * weights * (grad_weights - jnp.transpose(row_delta)[:, :, None])
    ).astype(jnp.bfloat16)
    grad_queries = jnp.einsum(
        "hit,tc->ihc", grad_scores, window, preferred_element_type=jnp.float32
    ).astype(jnp.bfloat16)
    return (weights_low, grad_scores, grad_queries)


def key_terms(weights_low, grad_scores, queries, grad_out, row_count):
    heads_dev, query_rows, window_rows = weights_low.shape
    block_rows = window_rows // (HOPS + 1)
    split_shape = (heads_dev, query_rows, HOPS + 1, block_rows)
    weight_part = weights_low.reshape(split_shape)
    score_part = grad_scores.reshape(split_shape)
    from_keys = jnp.einsum("hibt,ihc->tbc", score_part, queries, preferred_element_type=jnp.float32)
    from_values = jnp.einsum(
        "hibt,ihc->tbc", weight_part, grad_out, preferred_element_type=jnp.float32
    )
    merged = jnp.concatenate(
        [from_keys[:, :, :LATENT] + from_values, from_keys[:, :, LATENT:]], axis=2
    )
    return merged.reshape(row_count, (HOPS + 1) * queries.shape[2])


def local(queries, latent_cache, grad_out, segment_ids):
    tok_rows = latent_cache.shape[0]
    kv_width = latent_cache.shape[1]
    seq_index = lax.axis_index("seq")
    blocks = [latent_cache]
    moving = latent_cache
    for hop_index in range(HOPS):
        moving = shifted(moving, "seq", 1)
        blocks.append(moving)
    window = jnp.concatenate(blocks[::-1], axis=0)
    visible = window_mask(segment_ids, seq_index, tok_rows, window.shape[0])
    weights_low, grad_scores, grad_queries = attend(queries, window, grad_out, visible)
    partials = key_terms(weights_low, grad_scores, queries, grad_out, tok_rows)
    pieces = [
        partials[:, block_number * kv_width : (block_number + 1) * kv_width]
        for block_number in range(HOPS + 1)
    ]
    gathered_total = pieces[0]
    for hop_index in range(1, HOPS + 1):
        gathered_total = shifted(gathered_total, "seq", -1) + pieces[hop_index]
    grad_cache = lax.psum(gathered_total, "head").astype(jnp.bfloat16)
    return (grad_queries, grad_cache)


def solution(mesh):
    in_specs = (P("seq", "head", None), P("seq", None), P("seq", "head", None), P())
    out_specs = (P("seq", "head", None), P("seq", None))
    return jax.shard_map(local, mesh=mesh, in_specs=in_specs, out_specs=out_specs, check_vma=False)
```

profile of v0, /device:TPU:8, one launch (start us, length us, event | category | flops | bytes accessed | tf_op | source)
XLA Modules:
  0.0 91.8 jit_solution(11482344212733552853)
XLA Ops:
  0.6 0.0 copy-start
  0.6 0.0 copy-start.3
  0.7 0.0 copy-start.4
  0.7 2.1 %collective-permute-start = (bf16[128,576]{0,1:T(8,128)(2,1)}, bf16[128,576]{0,1:T(8,128)(2,1)S(1)}, u32[]{:S(2)}, u32[]{:S(2)}) collective-permute-start(bf16[128,576]{0,1:T(8,128)(2,1)} %param.5), channel_id=1, source_target_pairs={{0,8},{8,16},{16,24},{24,32},{32,40},{40,48},{48,56},{56,64},{64,7... | collective-permute-start | bytes 442376 | tf_op jit(solution)/shard_map/ppermute | solution.py:17
  2.7 4.5 %copy.8 = bf16[128,16,512]{0,2,1:T(8,128)(2,1)} copy(bf16[128,16,512]{2,1,0:T(8,128)(2,1)} %param.6) | data formatting | bytes 4194304 | tf_op args[2]
  7.3 0.0 copy-done.4
  7.3 0.1 dynamic_slice.6
  7.3 0.1 pad_dynamic-slice_fusion
  7.4 3.5 %collective-permute-done = bf16[128,576]{0,1:T(8,128)(2,1)S(1)} collective-permute-done((bf16[128,576]{0,1:T(8,128)(2,1)}, bf16[128,576]{0,1:T(8,128)(2,1)S(1)}, u32[]{:S(2)}, u32[]{:S(2)}) %collective-permute-start) | collective-permute-done | bytes 147488 | tf_op jit(solution)/shard_map/ppermute | solution.py:17
  10.9 1.9 %collective-permute-start.1 = (bf16[128,576]{0,1:T(8,128)(2,1)S(1)}, bf16[128,576]{0,1:T(8,128)(2,1)S(1)}, u32[]{:S(2)}, u32[]{:S(2)}) collective-permute-start(bf16[128,576]{0,1:T(8,128)(2,1)S(1)} %collective-permute-done), channel_id=1, source_target_pairs={{0,8},{8,16},{16,24},{24,32},{32,40},{40,48},{48,56},{56,64},{64,7... | collective-permute-start | bytes 442376 | tf_op jit(solution)/shard_map/ppermute | solution.py:17
  12.8 0.1 fusion.25
  13.0 6.5 %collective-permute-done.1 = bf16[128,576]{0,1:T(8,128)(2,1)S(1)} collective-permute-done((bf16[128,576]{0,1:T(8,128)(2,1)S(1)}, bf16[128,576]{0,1:T(8,128)(2,1)S(1)}, u32[]{:S(2)}, u32[]{:S(2)}) %collective-permute-start.1) | collective-permute-done | bytes 147488 | tf_op jit(solution)/shard_map/ppermute | solution.py:17
  19.6 0.0 copy-done.3
  19.6 0.0 copy-done
  19.6 1.4 %fusion.23 = f32[384,128,16]{1,0,2:T(8,128)S(1)} fusion(bf16[128,16,576]{0,2,1:T(8,128)(2,1)S(1)} %copy-done, bf16[384,576]{0,1:T(8,128)(2,1)S(1)} %constant_dynamic-update-slice_fusion), kind=kOutput, calls=%fused_computation.24 | convolution fusion | flops 905969664 | bytes 5947392 | tf_op jit(solution)/shard_map/ihc,tc->hit/dot_general | solution.py:34
  21.0 1.2 %fusion.28 = (f32[16,128]{1,0:T(8,128)S(1)}, f32[16,128,384]{1,2,0:T(8,128)S(1)}) fusion(f32[384,128,16]{1,0,2:T(8,128)S(1)} %fusion.23, pred[128,384]{0,1:T(8,128)(4,1)S(1)} %fusion.25), kind=kOutput, calls=%fused_computation.38 | output fusion | flops 5505407 | bytes 6348800 | tf_op jit(solution)/shard_map/sub | solution.py:38
  22.3 0.0 copy-start.2
  22.3 0.4 fusion.18
  22.7 1.2 %copy-done.2 = bf16[128,16,512]{0,2,1:T(8,128)(2,1)S(1)} copy-done((bf16[128,16,512]{0,2,1:T(8,128)(2,1)S(1)}, bf16[128,16,512]{0,2,1:T(8,128)(2,1)}, u32[]{:S(2)}) %copy-start.2) | copy-done | bytes 2097176
  23.9 1.3 %fusion.1 = f32[128,16]{0,1:T(8,128)S(1)} fusion(bf16[128,16,512]{0,2,1:T(8,128)(2,1)S(1)} %copy-done.2, bf16[16,128,384]{1,2,0:T(8,128)(2,1)S(1)} %fusion.18, bf16[384,576]{0,1:T(8,128)(2,1)S(1)} %constant_dynamic-update-slice_fusion), kind=kOutput, calls=%fused_computation.2 | convolution fusion | flops 808450048 | bytes 4071424 | tf_op jit(solution)/shard_map/hit,tc->ihc/dot_general | solution.py:41
  25.1 1.2 %fusion.3 = bf16[16,128,384]{1,2,0:T(8,128)(2,1)S(1)} fusion(bf16[128,16,512]{0,2,1:T(8,128)(2,1)S(1)} %copy-done.2, f32[16,128]{1,0:T(8,128)S(1)} %bitcast.67, f32[16,128,384]{1,2,0:T(8,128)S(1)} %get-tuple-element.3, f32[16,128]{1,0:T(8,128)S(1)} %get-tuple-element.2, bf16[384,576]{0,1:T(8,128)(2,1)S(1)} %constant_dynamic-update-slice_fusion), kind=kOutput, calls=%fused_computation.5 | convolution fusion | flops 809238528 | bytes 7225344 | tf_op jit(solution)/shard_map/ihc,tc->hit/dot_general | solution.py:43
  26.4 0.0 copy-start.1
  26.4 1.4 %fusion.12 = f32[128,3,576]{0,2,1:T(8,128)S(1)} fusion(bf16[16,128,3,128]{1,3,2,0:T(8,128)(2,1)S(1)} %bitcast.66, bf16[128,16,576]{0,2,1:T(8,128)(2,1)S(1)} %copy-done), kind=kOutput, calls=%fused_computation.18 | convolution fusion | flops 905969664 | bytes 4816896 | tf_op jit(solution)/shard_map/hibt,ihc->tbc/dot_general | solution.py:59
  27.8 0.2 copy-done.1
  28.0 2.4 %fusion.19 = f32[128,3,512]{0,2,1:T(8,128)S(1)} fusion(bf16[16,128,3,128]{1,3,2,0:T(8,128)(2,1)S(1)} %bitcast.65, bf16[128,16,512,1]{2,1,0,3:T(8,128)(2,1)S(1)} %bitcast.64, f32[128,3,576]{0,2,1:T(8,128)S(1)} %fusion.12), kind=kOutput, calls=%fused_computation.21 | convolution fusion | flops 805502976 | bytes 5242880 | tf_op jit(solution)/shard_map/hibt,ihc->tbc/dot_general | solution.py:60
  30.4 0.1 pad_maximum_fusion
  30.5 1.9 %collective-permute-start.2 = (f32[128,576]{0,1:T(8,128)S(1)}, f32[128,576]{0,1:T(8,128)S(1)}, u32[]{:S(2)}, u32[]{:S(2)}) collective-permute-start(f32[128,576]{0,1:T(8,128)S(1)} %slice.27), channel_id=1, source_target_pairs={{8,0},{16,8},{24,16},{32,24},{40,32},{48,40},{56,48},{64,56},{72,6... | collective-permute-start | bytes 884744 | tf_op jit(solution)/shard_map/ppermute | solution.py:17
  32.4 4.2 %collective-permute-done.2 = f32[128,576]{0,1:T(8,128)S(1)} collective-permute-done((f32[128,576]{0,1:T(8,128)S(1)}, f32[128,576]{0,1:T(8,128)S(1)}, u32[]{:S(2)}, u32[]{:S(2)}) %collective-permute-start.2) | collective-permute-done | bytes 294944 | tf_op jit(solution)/shard_map/ppermute | solution.py:17
  36.6 5.9 %collective-permute-start.3 = (f32[128,576]{0,1:T(8,128)S(1)}, f32[128,576]{0,1:T(8,128)S(1)}, u32[]{:S(2)}, u32[]{:S(2)}) collective-permute-start(f32[128,576]{0,1:T(8,128)S(1)} %slice_add_fusion.1), channel_id=1, source_target_pairs={{8,0},{16,8},{24,16},{32,24},{40,32},{48,40},{56,48},{64,56},{72,6... | collective-permute-start | bytes 884744 | tf_op jit(solution)/shard_map/ppermute | solution.py:17
  42.6 2.8 %convert_bitcast_fusion = bf16[128,16,576]{0,2,1:T(8,128)(2,1)} fusion(bf16[16,128,384]{1,2,0:T(8,128)(2,1)S(1)} %fusion.3, bf16[384,576]{0,1:T(8,128)(2,1)S(1)} %constant_dynamic-update-slice_fusion), kind=kOutput, calls=%fused_computation.11 | convolution fusion | flops 907149312 | bytes 4374528 | tf_op jit(solution)/shard_map/hit,tc->ihc/dot_general | solution.py:47
  45.4 1.6 %collective-permute-done.3 = f32[128,576]{0,1:T(8,128)S(1)} collective-permute-done((f32[128,576]{0,1:T(8,128)S(1)}, f32[128,576]{0,1:T(8,128)S(1)}, u32[]{:S(2)}, u32[]{:S(2)}) %collective-permute-start.3) | collective-permute-done | bytes 294944 | tf_op jit(solution)/shard_map/ppermute | solution.py:17
  47.0 44.8 %all-reduce.2 = bf16[128,576]{0,1:T(8,128)(2,1)} all-reduce(f32[128,576]{0,1:T(8,128)S(1)} %slice_add_fusion), channel_id=1, replica_groups=mesh['seq'=32,'head'=8] {'head'}, use_global_device_ids=true, to_apply=%region_3.4 | all-reduce | flops 73728 | bytes 442368 | tf_op jit(solution)/shard_map/psum | solution.py:89
  (8 shorter events, 0.2 us)
Async XLA Ops:
  0.6 19.0 %copy-start = (bf16[128,16,576]{0,2,1:T(8,128)(2,1)S(1)}, bf16[128,16,576]{0,2,1:T(8,128)(2,1)}, u32[]{:S(2)}) copy-start(bf16[128,16,576]{0,2,1:T(8,128)(2,1)} %param.4) | copy-start | bytes 7077892
  0.6 18.9 %copy-start.3 = (bf16[128,576]{0,1:T(8,128)(2,1)S(1)}, bf16[128,576]{0,1:T(8,128)(2,1)}, u32[]{:S(2)}) copy-start(bf16[128,576]{0,1:T(8,128)(2,1)} %param.5) | copy-start | bytes 442372
  0.7 6.6 %copy-start.4 = (s32[4096]{0:T(1024)S(1)}, s32[4096]{0:T(1024)}, u32[]{:S(2)}) copy-start(s32[4096]{0:T(1024)} %param.7) | copy-start | bytes 49156
  0.7 10.3 %collective-permute-start = (bf16[128,576]{0,1:T(8,128)(2,1)}, bf16[128,576]{0,1:T(8,128)(2,1)S(1)}, u32[]{:S(2)}, u32[]{:S(2)}) collective-permute-start(bf16[128,576]{0,1:T(8,128)(2,1)} %param.5), channel_id=1, source_target_pairs={{0,8},{8,16},{16,24},{24,32},{32,40},{40,48},{48,56},{56,64},{64,7... | collective-permute-start | bytes 442376 | tf_op jit(solution)/shard_map/ppermute | solution.py:17
  10.9 8.6 %collective-permute-start.1 = (bf16[128,576]{0,1:T(8,128)(2,1)S(1)}, bf16[128,576]{0,1:T(8,128)(2,1)S(1)}, u32[]{:S(2)}, u32[]{:S(2)}) collective-permute-start(bf16[128,576]{0,1:T(8,128)(2,1)S(1)} %collective-permute-done), channel_id=1, source_target_pairs={{0,8},{8,16},{16,24},{24,32},{32,40},{40,48},{48,56},{56,64},{64,7... | collective-permute-start | bytes 442376 | tf_op jit(solution)/shard_map/ppermute | solution.py:17
  22.3 1.6 %copy-start.2 = (bf16[128,16,512]{0,2,1:T(8,128)(2,1)S(1)}, bf16[128,16,512]{0,2,1:T(8,128)(2,1)}, u32[]{:S(2)}) copy-start(bf16[128,16,512]{0,2,1:T(8,128)(2,1)} %copy.8) | copy-start | bytes 6291460
  26.4 1.6 %copy-start.1 = (bf16[128,16,512]{2,1,0:T(8,128)(2,1)S(1)}, bf16[128,16,512]{2,1,0:T(8,128)(2,1)}, u32[]{:S(2)}) copy-start(bf16[128,16,512]{2,1,0:T(8,128)(2,1)} %param.6) | copy-start | bytes 6291460
  30.5 6.1 %collective-permute-start.2 = (f32[128,576]{0,1:T(8,128)S(1)}, f32[128,576]{0,1:T(8,128)S(1)}, u32[]{:S(2)}, u32[]{:S(2)}) collective-permute-start(f32[128,576]{0,1:T(8,128)S(1)} %slice.27), channel_id=1, source_target_pairs={{8,0},{16,8},{24,16},{32,24},{40,32},{48,40},{56,48},{64,56},{72,6... | collective-permute-start | bytes 884744 | tf_op jit(solution)/shard_map/ppermute | solution.py:17
  36.6 10.3 %collective-permute-start.3 = (f32[128,576]{0,1:T(8,128)S(1)}, f32[128,576]{0,1:T(8,128)S(1)}, u32[]{:S(2)}, u32[]{:S(2)}) collective-permute-start(f32[128,576]{0,1:T(8,128)S(1)} %slice_add_fusion.1), channel_id=1, source_target_pairs={{8,0},{16,8},{24,16},{32,24},{40,32},{48,40},{56,48},{64,56},{72,6... | collective-permute-start | bytes 884744 | tf_op jit(solution)/shard_map/ppermute | solution.py:17
where the time goes:
time: 92.2 us; the launch traced here: 91.8 us
  blocking collectives  44.8 us (49%)
  waiting for transfers between devices  15.8 us (17%)
  starting transfers between devices  11.8 us (13%)
  matrix products  10.5 us (11%)
  local copies, waits for them, and re-layouts  6.19 us (7%)
  other arithmetic  1.85 us (2%)
    psum x1, blocking collectives, local(): grad_cache = lax.psum(gathered_total, 'head').astype(jnp.bfloat16)  44.8 us
    ppermute x4, waiting for transfers between devices, shifted(): return lax.ppermute(block, axis, route)  15.8 us
    ppermute x4, starting transfers between devices, shifted(): return lax.ppermute(block, axis, route)  11.8 us
    unnamed x13, local copies, waits for them, and re-layouts  5.97 us
    dot_general x1, matrix products, attend(): jnp.einsum('hit,tc->ihc', grad_scores, window, preferred_element_type=jnp...  2.81 us
    dot_general x1, matrix products, key_terms(): jnp.einsum('hibt,ihc->tbc', weight_part, grad_out, preferred_element_type...  2.37 us
  transfers between devices with their start and end apart: 4, of which 4 were waited for; matrix products, arithmetic and copies ran while one was open for 8% of the time, Pallas kernels for 0%

commit v1 on v0

v1 whole, which is shorter than its diff:
```python
import functools

import jax
import jax.numpy as jnp
from jax import lax
from jax.experimental import pallas as pl
from jax.experimental.pallas import tpu as pltpu
from jax.sharding import PartitionSpec as P

MESH = pl.DeviceIdType.MESH
LATENT = 512
N_X = 4
score_scale = 192.0 ** (-0.5)
exp2_scale = score_scale * 1.4426950408889634
masked_score = -1e30
bf16 = jnp.bfloat16
f32 = jnp.float32


def dot(a, b):
    return lax.dot_general(a, b, (((1,), (0,)), ((), ())), preferred_element_type=f32)


def dot_nt(a, b):
    return lax.dot_general(a, b, (((1,), (1,)), ((), ())), preferred_element_type=f32)


def kernel(n_seq, n_head, q_hbm, kt_hbm, do_hbm, seg_hbm, dq_hbm, gc_ref,
           q, kt, kk, do, doh, dot_, seg, s0, g0, p_all, ds_all, dq, mask,
           psend, pown, rbuf, gbuf,
           lsem, osem, wsend, wrecv, psems, precv, gsend, grecv, ready):
    heads, kv, tok = q.shape
    pairs = heads // 2
    quarter = kv // N_X
    s = lax.axis_index("seq")
    h = lax.axis_index("head")
    x, y = h // 2, h % 2

    load_k = pltpu.make_async_copy(kt_hbm, kt.at[2], lsem.at[0])
    load_s = pltpu.make_async_copy(seg_hbm, seg, lsem.at[1])
    load_do = pltpu.make_async_copy(do_hbm, do, lsem.at[2])
    load_q = pltpu.make_async_copy(q_hbm, q, lsem.at[3])
    for c in (load_k, load_s, load_do, load_q):
        c.start()

    barrier = pltpu.get_barrier_semaphore()
    for d in (1, 2):
        @pl.when(s + d < n_seq)
        def _():
            pl.semaphore_signal(barrier, inc=1, device_id={"seq": s + d, "head": h}, device_id_type=MESH)

        @pl.when(s - d >= 0)
        def _():
            pl.semaphore_signal(barrier, inc=1, device_id={"seq": s - d, "head": h}, device_id_type=MESH)
    for d in range(1, n_head):
        pl.semaphore_signal(barrier, inc=1, device_id={"seq": s, "head": (h + d) % n_head}, device_id_type=MESH)
    ahead = jnp.minimum(n_seq - 1 - s, 2)
    behind = jnp.minimum(s, 2)
    pl.semaphore_wait(barrier, ahead + behind + n_head - 1)

    win = [
        pltpu.make_async_remote_copy(
            src_ref=kt_hbm, dst_ref=kt.at[2 - d], send_sem=wsend.at[d - 1], recv_sem=wrecv.at[d - 1],
            device_id={"seq": s + d, "head": h}, device_id_type=MESH)
        for d in (1, 2)
    ]
    for d in (1, 2):
        @pl.when(s + d < n_seq)
        def _():
            win[d - 1].start()

        @pl.when(s - d < 0)
        def _():
            kt[2 - d] = jnp.zeros((kv, tok), bf16)

        @pl.when(s + d >= n_seq)
        def _():
            for j in range(N_X):
                rbuf[(d - 1) * N_X + j] = jnp.zeros((quarter, tok), bf16)

    load_s.wait()
    row = lax.broadcasted_iota(jnp.int32, (tok, tok), 0)
    col = lax.broadcasted_iota(jnp.int32, (tok, tok), 1)
    tri = row <= col
    seg_q = jnp.broadcast_to(seg[pl.ds(s, 1), :], (tok, tok))

    def key_seg(d):
        line = jnp.broadcast_to(seg[pl.ds(jnp.maximum(s - d, 0), 1), :], (tok, tok))
        line = jnp.where(s - d >= 0, line, -1)
        return jnp.transpose(line)

    seen_p = jnp.where(tri, key_seg(0), key_seg(2)) == seg_q
    seen_1 = key_seg(1) == seg_q
    mask[0] = jnp.where(seen_1, 0.0, masked_score)
    mask[1] = jnp.where(seen_p, 0.0, masked_score)

    load_k.wait()
    kk[pl.ds(2 * tok, tok), :] = jnp.transpose(kt[2])
    load_do.wait()
    r = lax.broadcasted_iota(jnp.int32, (256, 256), 0)
    c = lax.broadcasted_iota(jnp.int32, (256, 256), 1)
    perm = ((r // 16 == c % 16) & (r % 16 == c // 16)).astype(bf16)
    for i in range(tok // 16):
        part = dot(perm, do[pl.ds(i * 256, 256), :]).astype(bf16)
        for hh in range(heads):
            doh[hh, pl.ds(i * 16, 16), :] = part[hh * 16:(hh + 1) * 16]
    for hh in range(heads):
        dot_[hh] = jnp.transpose(doh[hh])
    load_q.wait()

    def pair(ref, p):
        return jnp.concatenate([ref[2 * p], ref[2 * p + 1]], axis=1)

    for p in range(pairs):
        lanes = pl.ds(p * 256, 256)
        s0[:, lanes] = dot(kk[pl.ds(2 * tok, tok), :], pair(q, p))
        g0[:, lanes] = dot(kk[pl.ds(2 * tok, tok), :LATENT], pair(dot_, p))

    for d in (1, 2):
        @pl.when(s - d >= 0)
        def _():
            win[d - 1].wait_recv()
        kk[pl.ds((2 - d) * tok, tok), :] = jnp.transpose(kt[2 - d])
    for d in range(1, N_X):
        pl.semaphore_signal(ready, inc=1, device_id={"seq": s, "head": (h + 2 * d) % n_head}, device_id_type=MESH)

    tri2 = jnp.concatenate([tri, tri], axis=1)
    m1 = jnp.concatenate([mask[0], mask[0]], axis=1)
    mp = jnp.concatenate([mask[1], mask[1]], axis=1)
    for p in range(pairs):
        lanes = pl.ds(p * 256, 256)
        s12 = dot(kk[pl.ds(0, 2 * tok), :], pair(q, p))
        g12 = dot(kk[pl.ds(0, 2 * tok), :LATENT], pair(dot_, p))
        sp = jnp.where(tri2, s0[:, lanes], s12[:tok]) + mp
        s1 = s12[tok:] + m1
        top = jnp.maximum(jnp.max(sp, axis=0, keepdims=True), jnp.max(s1, axis=0, keepdims=True))
        ep = jnp.exp2((sp - top) * exp2_scale)
        e1 = jnp.exp2((s1 - top) * exp2_scale)
        inv = 1.0 / (jnp.sum(ep, axis=0, keepdims=True) + jnp.sum(e1, axis=0, keepdims=True))
        wp, w1 = ep * inv, e1 * inv
        wlp, wl1 = wp.astype(bf16), w1.astype(bf16)
        gp, g1 = jnp.where(tri2, g0[:, lanes], g12[:tok]), g12[tok:]
        delta = (jnp.sum(wlp.astype(f32) * gp, axis=0, keepdims=True)
                 + jnp.sum(wl1.astype(f32) * g1, axis=0, keepdims=True))
        dsp = (score_scale * wp * (gp - delta)).astype(bf16)
        ds1 = (score_scale * w1 * (g1 - delta)).astype(bf16)
        zero = jnp.zeros_like(wlp)
        p_all[0:tok, lanes] = jnp.where(tri2, zero, wlp)
        p_all[tok:2 * tok, lanes] = wl1
        p_all[2 * tok:, lanes] = jnp.where(tri2, wlp, zero)
        ds_all[0:tok, lanes] = jnp.where(tri2, zero, dsp)
        ds_all[tok:2 * tok, lanes] = ds1
        ds_all[2 * tok:, lanes] = jnp.where(tri2, dsp, zero)

    qall = jnp.concatenate([q[hh] for hh in range(heads)], axis=1)
    dall = jnp.concatenate([dot_[hh] for hh in range(heads)], axis=1)

    def key_grad(rows):
        from_keys = dot_nt(qall, ds_all[rows, :])
        from_values = dot_nt(dall, p_all[rows, :])
        return from_keys[:LATENT] + from_values, from_keys[LATENT:]

    low, high = key_grad(pl.ds(0, 2 * tok))
    for b in (0, 1):
        psend[b, :LATENT, :] = low[:, b * tok:(b + 1) * tok].astype(bf16)
        psend[b, LATENT:, :] = high[:, b * tok:(b + 1) * tok].astype(bf16)
    pl.semaphore_wait(ready, N_X - 1)

    def part_copy(b, j):
        xx = (x + j) % N_X
        slot = (1 - b) * N_X + j if b < 2 else 2 * N_X + j - 1
        return pltpu.make_async_remote_copy(
            src_ref=psend.at[b, pl.ds(pl.multiple_of(xx * quarter, 16), quarter)],
            dst_ref=rbuf.at[slot], send_sem=psems.at[slot], recv_sem=precv.at[slot],
            device_id={"seq": s - (2 - b), "head": xx * 2 + y}, device_id_type=MESH)

    for b in (0, 1):
        @pl.when(s >= 2 - b)
        def _():
            for j in (2, 1, 3, 0):
                part_copy(b, j).start()

    low, high = key_grad(pl.ds(2 * tok, tok))
    psend[2, :LATENT, :] = low.astype(bf16)
    psend[2, LATENT:, :] = high.astype(bf16)
    for j in (2, 1, 3):
        part_copy(2, j).start()
    pown[:LATENT, :] = low
    pown[LATENT:, :] = high

    ktall = jnp.concatenate([kt[0], kt[1], kt[2]], axis=1)
    for p in range(pairs):
        out = dot(ktall, ds_all[:, pl.ds(p * 256, 256)]).astype(bf16)
        dq[2 * p] = out[:, :tok]
        dq[2 * p + 1] = out[:, tok:]
    store = pltpu.make_async_copy(dq, dq_hbm, osem)
    store.start()

    total = pown[pl.ds(pl.multiple_of(x * quarter, 16), quarter), :]
    for b in (2, 1, 0):
        for j in range(1 if b == 2 else 0, N_X):
            if b == 2:
                part_copy(b, j).wait_recv()
            else:
                @pl.when(s + 2 - b < n_seq)
                def _():
                    part_copy(b, j).wait_recv()
            slot = (1 - b) * N_X + j if b < 2 else 2 * N_X + j - 1
            total = total + rbuf[slot].astype(f32)
    mine = pl.ds(pl.multiple_of(x * quarter, 16), quarter)
    gbuf[y, mine, :] = total.astype(bf16)

    def gather_copy(d):
        return pltpu.make_async_remote_copy(
            src_ref=gbuf.at[y, mine], dst_ref=gbuf.at[y, mine],
            send_sem=gsend.at[d - 1], recv_sem=grecv.at[d - 1],
            device_id={"seq": s, "head": (h + d) % n_head}, device_id_type=MESH)

    for d in (3, 5, 4, 1, 7, 2, 6):
        gather_copy(d).start()
    for d in (2, 6, 1, 7, 4, 3, 5):
        gather_copy(d).wait_recv()
    gc_ref[...] = (gbuf[0].astype(f32) + gbuf[1].astype(f32)).astype(bf16)

    for d in (1, 2):
        @pl.when(s + d < n_seq)
        def _():
            win[d - 1].wait_send()
    for b in (0, 1):
        @pl.when(s >= 2 - b)
        def _():
            for j in range(N_X):
                part_copy(b, j).wait_send()
    for j in range(1, N_X):
        part_copy(2, j).wait_send()
    for d in range(1, n_head):
        gather_copy(d).wait_send()
    store.wait()


def local(n_seq, n_head, queries, latent_cache, grad_out, segment_ids):
    tok, heads, kv = queries.shape
    q = jnp.transpose(queries, (1, 2, 0))
    kt = jnp.transpose(latent_cache)
    do = grad_out.reshape(tok * heads, LATENT)
    seg = segment_ids.reshape(n_seq, tok)
    rows = tok * heads
    quarter = kv // N_X
    dma = pltpu.SemaphoreType.DMA
    anywhere = pl.BlockSpec(memory_space=pl.ANY)
    dq, gc = pl.pallas_call(
        functools.partial(kernel, n_seq, n_head),
        out_shape=(jax.ShapeDtypeStruct((heads, kv, tok), bf16), jax.ShapeDtypeStruct((kv, tok), bf16)),
        in_specs=[anywhere] * 4,
        out_specs=(anywhere, pl.BlockSpec(memory_space=pltpu.VMEM)),
        scratch_shapes=[
            pltpu.VMEM((heads, kv, tok), bf16),
            pltpu.VMEM((3, kv, tok), bf16),
            pltpu.VMEM((3 * tok, kv), bf16),
            pltpu.VMEM((rows, LATENT), bf16),
            pltpu.VMEM((heads, tok, LATENT), bf16),
            pltpu.VMEM((heads, LATENT, tok), bf16),
            pltpu.VMEM((n_seq, tok), jnp.int32),
            pltpu.VMEM((tok, rows), f32),
            pltpu.VMEM((tok, rows), f32),
            pltpu.VMEM((3 * tok, rows), bf16),
            pltpu.VMEM((3 * tok, rows), bf16),
            pltpu.VMEM((heads, kv, tok), bf16),
            pltpu.VMEM((2, tok, tok), f32),
            pltpu.VMEM((3, kv, tok), bf16),
            pltpu.VMEM((kv, tok), f32),
            pltpu.VMEM((3 * N_X - 1, quarter, tok), bf16),
            pltpu.VMEM((2, kv, tok), bf16),
            dma((4,)), dma, dma((2,)), dma((2,)),
            dma((3 * N_X - 1,)), dma((3 * N_X - 1,)), dma((n_head - 1,)), dma((n_head - 1,)),
            pltpu.SemaphoreType.REGULAR,
        ],
        compiler_params=pltpu.CompilerParams(
            collective_id=0, has_side_effects=True, vmem_limit_bytes=50 << 20),
        cost_estimate=pl.CostEstimate(flops=6 * 10**9, bytes_accessed=8 * 10**6, transcendentals=10**6),
        name="latent_backward",
    )(q, kt, do, seg)
    return jnp.transpose(dq, (2, 0, 1)), jnp.transpose(gc)


def solution(mesh):
    in_specs = (P("seq", "head", None), P("seq", None), P("seq", "head", None), P())
    out_specs = (P("seq", "head", None), P("seq", None))
    return jax.shard_map(
        functools.partial(local, mesh.shape["seq"], mesh.shape["head"]),
        mesh=mesh, in_specs=in_specs, out_specs=out_specs, check_vma=False)
```

time: 92.2 us -> 42 us (0.46)
  blocking collectives: 44.8 us -> 0 us
  Pallas kernels: 0 us -> 33.8 us
  waiting for transfers between devices: 15.8 us -> 0 us
  starting transfers between devices: 11.8 us -> 0 us
  matrix products: 10.5 us -> 0 us
  other arithmetic: 1.85 us -> 0 us
    psum x1 -> x0, blocking collectives: 44.8 us -> none  [local(): grad_cache = lax.psum(gathered_total, 'head').astype(jnp.bfloat16)]
    pallas_call x0 -> x1, Pallas kernels: none -> 33.8 us  [local(): pl.pallas_call(functools.partial(kernel, n_seq, n_head), out_shape=(jax.S...]
    ppermute x4 -> x0, waiting for transfers between devices: 15.8 us -> none  [shifted(): return lax.ppermute(block, axis, route)]
    ppermute x4 -> x0, starting transfers between devices: 11.8 us -> none  [shifted(): return lax.ppermute(block, axis, route)]
    dot_general x6 -> x0, matrix products: 10.5 us -> none  [the longest x1 2.81 us: attend(): jnp.einsum('hit,tc->ihc', grad_scores, window, preferred_element_type=jnp...]
    sub x1 -> x0, other arithmetic: 1.23 us -> none  [attend(): expo_terms = jnp.where(visible[None], jnp.exp(scores - row_max), 0.0)]
    unnamed x13 -> x8, local copies, waits for them, and re-layouts: 5.97 us -> 7.11 us
  transfers between devices with their start and end apart: 4 -> 0, of which waited for: 4 -> 0; matrix products, arithmetic and copies ran while one was open for 8% -> 0% of each run, Pallas kernels for 0% -> 0%
where the time goes in v1:
time: 42 us; the launch traced here: 41.6 us
  Pallas kernels  33.8 us (80%)
  local copies, waits for them, and re-layouts  7.11 us (17%)
  between operations  0.65 us (2%)
    pallas_call x1, Pallas kernels, local(): pl.pallas_call(functools.partial(kernel, n_seq, n_head), out_shape=(jax.S...  33.8 us
    unnamed x8, local copies, waits for them, and re-layouts  7.11 us

profile of v1, /device:TPU:8, one launch (start us, length us, event | category | flops | bytes accessed | tf_op | source)
XLA Modules:
  0.0 41.6 jit_solution(3859754471461295809)
XLA Ops:
  0.6 0.0 copy-start
  0.6 1.6 %copy-done = bf16[128,16,512]{2,1,0:T(8,128)(2,1)S(1)} copy-done((bf16[128,16,512]{2,1,0:T(8,128)(2,1)S(1)}, bf16[128,16,512]{2,1,0:T(8,128)(2,1)}, u32[]{:S(2)}) %copy-start) | copy-done | bytes 2097176
  2.2 0.0 copy-start.1
  2.2 0.9 %copy-done.1 = bf16[128,576]{0,1:T(8,128)(2,1)S(1)} copy-done((bf16[128,576]{0,1:T(8,128)(2,1)S(1)}, bf16[128,576]{0,1:T(8,128)(2,1)}, u32[]{:S(2)}) %copy-start.1) | copy-done | bytes 147480
  3.1 0.0 copy-start.2
  3.1 0.7 %copy-done.2 = s32[4096]{0:T(1024)S(1)} copy-done((s32[4096]{0:T(1024)S(1)}, s32[4096]{0:T(1024)}, u32[]{:S(2)}) %copy-start.2) | copy-done | bytes 16408
  3.9 33.8 %latent_backward.1 = (bf16[16,576,128]{2,1,0:T(8,128)(2,1)}, bf16[576,128]{1,0:T(8,128)(2,1)S(1)}) custom-call(bf16[16,576,128]{2,1,0:T(8,128)(2,1)} %bitcast.11, bf16[576,128]{1,0:T(8,128)(2,1)S(1)} %bitcast.8, bf16[2048,512]{1,0:T(8,128)(2,1)S(1)} %bitcast.7, s32[32,128]{1,0:T(8,128)S(1)} %bitcast.9), custom_call_target="tpu_custom_call" | custom-call | flops 6000000000 | bytes 8000000 | tf_op jit(solution)/shard_map/latent_backward/pallas_call | solution.py:251
  37.7 3.2 %copy.8 = bf16[128,16,576]{0,2,1:T(8,128)(2,1)} copy(bf16[128,16,576]{0,2,1:T(8,128)(2,1)} %bitcast.10) | data formatting | bytes 4718592
  40.9 0.7 %copy.9 = bf16[128,576]{0,1:T(8,128)(2,1)} copy(bf16[128,576]{0,1:T(8,128)(2,1)S(1)} %bitcast.6) | data formatting | bytes 294912
Async XLA Ops:
  0.6 1.6 %copy-start = (bf16[128,16,512]{2,1,0:T(8,128)(2,1)S(1)}, bf16[128,16,512]{2,1,0:T(8,128)(2,1)}, u32[]{:S(2)}) copy-start(bf16[128,16,512]{2,1,0:T(8,128)(2,1)} %param.6) | copy-start | bytes 6291460
  2.2 0.9 %copy-start.1 = (bf16[128,576]{0,1:T(8,128)(2,1)S(1)}, bf16[128,576]{0,1:T(8,128)(2,1)}, u32[]{:S(2)}) copy-start(bf16[128,576]{0,1:T(8,128)(2,1)} %param.5) | copy-start | bytes 442372
  3.1 0.7 %copy-start.2 = (s32[4096]{0:T(1024)S(1)}, s32[4096]{0:T(1024)}, u32[]{:S(2)}) copy-start(s32[4096]{0:T(1024)} %param.7) | copy-start | bytes 49156

commit v2 on v1

--- a/solution.py
+++ b/solution.py
@@ -25,23 +25,24 @@
     return lax.dot_general(a, b, (((1,), (1,)), ((), ())), preferred_element_type=f32)
 
 
-def kernel(n_seq, n_head, q_hbm, kt_hbm, do_hbm, seg_hbm, dq_hbm, gc_ref,
-           q, kt, kk, do, doh, dot_, seg, s0, g0, p_all, ds_all, dq, mask,
-           psend, pown, rbuf, gbuf,
-           lsem, osem, wsend, wrecv, psems, precv, gsend, grecv, ready):
+def kernel(n_seq, n_head, q_hbm, kt_hbm, do_hbm, seg_hbm, dq, gc_ref,
+           q, kt, kk, do, doh, qn, dot_, seg, s0, g0, p_all, ds_all, mask,
+           pmid, psend, pown, pacc, rbuf, gbuf,
+           lsem, wsend, wrecv, msem, psems, precv, gsend, grecv, ready):
     heads, kv, tok = q.shape
     pairs = heads // 2
     quarter = kv // N_X
     s = lax.axis_index("seq")
     h = lax.axis_index("head")
     x, y = h // 2, h % 2
+    core = s % 2
 
     load_k = pltpu.make_async_copy(kt_hbm, kt.at[2], lsem.at[0])
     load_s = pltpu.make_async_copy(seg_hbm, seg, lsem.at[1])
     load_do = pltpu.make_async_copy(do_hbm, do, lsem.at[2])
     load_q = pltpu.make_async_copy(q_hbm, q, lsem.at[3])
-    for c in (load_k, load_s, load_do, load_q):
-        c.start()
+    load_k.start()
+    load_s.start()
 
     barrier = pltpu.get_barrier_semaphore()
     for d in (1, 2):
@@ -64,7 +65,7 @@
             device_id={"seq": s + d, "head": h}, device_id_type=MESH)
         for d in (1, 2)
     ]
-    for d in (1, 2):
+    for d in (2, 1):
         @pl.when(s + d < n_seq)
         def _():
             win[d - 1].start()
@@ -73,10 +74,13 @@
         def _():
             kt[2 - d] = jnp.zeros((kv, tok), bf16)
 
-        @pl.when(s + d >= n_seq)
-        def _():
-            for j in range(N_X):
-                rbuf[(d - 1) * N_X + j] = jnp.zeros((quarter, tok), bf16)
+    @pl.when(s + 2 >= n_seq)
+    def _():
+        for j in range(N_X):
+            rbuf[j] = jnp.zeros((quarter, tok), bf16)
+
+    load_do.start()
+    load_q.start()
 
     load_s.wait()
     row = lax.broadcasted_iota(jnp.int32, (tok, tok), 0)
@@ -103,9 +107,9 @@
     for i in range(tok // 16):
         part = dot(perm, do[pl.ds(i * 256, 256), :]).astype(bf16)
         for hh in range(heads):
-            doh[hh, pl.ds(i * 16, 16), :] = part[hh * 16:(hh + 1) * 16]
+            doh[pl.ds(hh * tok + i * 16, 16), :] = part[hh * 16:(hh + 1) * 16]
     for hh in range(heads):
-        dot_[hh] = jnp.transpose(doh[hh])
+        dot_[hh] = jnp.transpose(doh[pl.ds(hh * tok, tok), :])
     load_q.wait()
 
     def pair(ref, p):
@@ -115,6 +119,9 @@
         lanes = pl.ds(p * 256, 256)
         s0[:, lanes] = dot(kk[pl.ds(2 * tok, tok), :], pair(q, p))
         g0[:, lanes] = dot(kk[pl.ds(2 * tok, tok), :LATENT], pair(dot_, p))
+
+    for hh in range(heads):
+        qn[pl.ds(hh * tok, tok), :] = jnp.transpose(q[hh])
 
     for d in (1, 2):
         @pl.when(s - d >= 0)
@@ -152,61 +159,75 @@
         ds_all[tok:2 * tok, lanes] = ds1
         ds_all[2 * tok:, lanes] = jnp.where(tri2, dsp, zero)
 
-    qall = jnp.concatenate([q[hh] for hh in range(heads)], axis=1)
-    dall = jnp.concatenate([dot_[hh] for hh in range(heads)], axis=1)
-
-    def key_grad(rows):
-        from_keys = dot_nt(qall, ds_all[rows, :])
-        from_values = dot_nt(dall, p_all[rows, :])
-        return from_keys[:LATENT] + from_values, from_keys[LATENT:]
-
-    low, high = key_grad(pl.ds(0, 2 * tok))
-    for b in (0, 1):
-        psend[b, :LATENT, :] = low[:, b * tok:(b + 1) * tok].astype(bf16)
-        psend[b, LATENT:, :] = high[:, b * tok:(b + 1) * tok].astype(bf16)
-    pl.semaphore_wait(ready, N_X - 1)
+    def key_grad(block):
+        rows = pl.ds(block * tok, tok)
+        pown[...] = dot(ds_all[rows, :], qn[...])
+        pown[:, :LATENT] += dot(p_all[rows, :], doh[...])
+        return pown[...]
+
+    swap = pltpu.make_async_remote_copy(
+        src_ref=pmid.at[0], dst_ref=pmid.at[1], send_sem=msem.at[0], recv_sem=msem.at[1],
+        device_id={"seq": s + 1 - 2 * core, "head": h}, device_id_type=MESH)
 
     def part_copy(b, j):
         xx = (x + j) % N_X
-        slot = (1 - b) * N_X + j if b < 2 else 2 * N_X + j - 1
+        slot = b * N_X + j - b
         return pltpu.make_async_remote_copy(
             src_ref=psend.at[b, pl.ds(pl.multiple_of(xx * quarter, 16), quarter)],
             dst_ref=rbuf.at[slot], send_sem=psems.at[slot], recv_sem=precv.at[slot],
-            device_id={"seq": s - (2 - b), "head": xx * 2 + y}, device_id_type=MESH)
-
-    for b in (0, 1):
-        @pl.when(s >= 2 - b)
-        def _():
-            for j in (2, 1, 3, 0):
-                part_copy(b, j).start()
-
-    low, high = key_grad(pl.ds(2 * tok, tok))
-    psend[2, :LATENT, :] = low.astype(bf16)
-    psend[2, LATENT:, :] = high.astype(bf16)
+            device_id={"seq": s - 2 * (1 - b), "head": xx * 2 + y}, device_id_type=MESH)
+
+    def middle():
+        pmid[0] = key_grad(1).astype(bf16)
+
+        @pl.when(s > 0)
+        def _():
+            swap.start()
+
+    @pl.when(core == 0)
+    def _():
+        pacc[...] = key_grad(2)
+        middle()
+        swap.wait_recv()
+        psend[1] = jnp.transpose((pacc[...] + pmid[1].astype(f32)).astype(bf16))
+
+    @pl.when(core == 1)
+    def _():
+        middle()
+        psend[1] = jnp.transpose(key_grad(2).astype(bf16))
+
+    pl.semaphore_wait(ready, N_X - 1)
     for j in (2, 1, 3):
-        part_copy(2, j).start()
-    pown[:LATENT, :] = low
-    pown[LATENT:, :] = high
+        part_copy(1, j).start()
+
+    @pl.when(s >= 2)
+    def _():
+        key_grad(0)
+
+        @pl.when(core == 1)
+        def _():
+            swap.wait_recv()
+            pown[...] += pmid[1].astype(f32)
+        psend[0] = jnp.transpose(pown[...].astype(bf16))
+        for j in (2, 1, 3, 0):
+            part_copy(0, j).start()
 
     ktall = jnp.concatenate([kt[0], kt[1], kt[2]], axis=1)
     for p in range(pairs):
         out = dot(ktall, ds_all[:, pl.ds(p * 256, 256)]).astype(bf16)
         dq[2 * p] = out[:, :tok]
         dq[2 * p + 1] = out[:, tok:]
-    store = pltpu.make_async_copy(dq, dq_hbm, osem)
-    store.start()
-
-    total = pown[pl.ds(pl.multiple_of(x * quarter, 16), quarter), :]
-    for b in (2, 1, 0):
-        for j in range(1 if b == 2 else 0, N_X):
-            if b == 2:
-                part_copy(b, j).wait_recv()
-            else:
-                @pl.when(s + 2 - b < n_seq)
-                def _():
-                    part_copy(b, j).wait_recv()
-            slot = (1 - b) * N_X + j if b < 2 else 2 * N_X + j - 1
-            total = total + rbuf[slot].astype(f32)
+
+
+    total = psend[1, pl.ds(pl.multiple_of(x * quarter, 16), quarter), :].astype(f32)
+    for j in range(1, N_X):
+        part_copy(1, j).wait_recv()
+        total = total + rbuf[N_X + j - 1].astype(f32)
+    for j in range(N_X):
+        @pl.when(s + 2 < n_seq)
+        def _():
+            part_copy(0, j).wait_recv()
+        total = total + rbuf[j].astype(f32)
     mine = pl.ds(pl.multiple_of(x * quarter, 16), quarter)
     gbuf[y, mine, :] = total.astype(bf16)
 
@@ -226,16 +247,26 @@
         @pl.when(s + d < n_seq)
         def _():
             win[d - 1].wait_send()
-    for b in (0, 1):
-        @pl.when(s >= 2 - b)
-        def _():
-            for j in range(N_X):
-                part_copy(b, j).wait_send()
+    @pl.when(s > 0)
+    def _():
+        swap.wait_send()
+
+    @pl.when(s >= 2)
+    def _():
+        for j in range(N_X):
+            part_copy(0, j).wait_send()
     for j in range(1, N_X):
-        part_copy(2, j).wait_send()
+        part_copy(1, j).wait_send()
     for d in range(1, n_head):
         gather_copy(d).wait_send()
-    store.wait()
+
+
+def store_kernel(dq, gc, dq_hbm, gc_hbm, sems):
+    copies = [pltpu.make_async_copy(gc, gc_hbm, sems.at[0]), pltpu.make_async_copy(dq, dq_hbm, sems.at[1])]
+    for c in copies:
+        c.start()
+    for c in copies:
+        c.wait()
 
 
 def local(n_seq, n_head, queries, latent_cache, grad_out, segment_ids):
@@ -247,39 +278,49 @@
     rows = tok * heads
     quarter = kv // N_X
     dma = pltpu.SemaphoreType.DMA
-    anywhere = pl.BlockSpec(memory_space=pl.ANY)
+    hbm = pl.BlockSpec(memory_space=pltpu.HBM)
     dq, gc = pl.pallas_call(
         functools.partial(kernel, n_seq, n_head),
-        out_shape=(jax.ShapeDtypeStruct((heads, kv, tok), bf16), jax.ShapeDtypeStruct((kv, tok), bf16)),
-        in_specs=[anywhere] * 4,
-        out_specs=(anywhere, pl.BlockSpec(memory_space=pltpu.VMEM)),
+        out_shape=(pltpu.VMEM((heads, kv, tok), bf16), pltpu.VMEM((kv, tok), bf16)),
+        in_specs=[hbm] * 4,
+        out_specs=(pl.BlockSpec(memory_space=pltpu.VMEM), pl.BlockSpec(memory_space=pltpu.VMEM)),
         scratch_shapes=[
             pltpu.VMEM((heads, kv, tok), bf16),
             pltpu.VMEM((3, kv, tok), bf16),
             pltpu.VMEM((3 * tok, kv), bf16),
             pltpu.VMEM((rows, LATENT), bf16),
-            pltpu.VMEM((heads, tok, LATENT), bf16),
+            pltpu.VMEM((rows, LATENT), bf16),
+            pltpu.VMEM((rows, kv), bf16),
             pltpu.VMEM((heads, LATENT, tok), bf16),
             pltpu.VMEM((n_seq, tok), jnp.int32),
             pltpu.VMEM((tok, rows), f32),
             pltpu.VMEM((tok, rows), f32),
             pltpu.VMEM((3 * tok, rows), bf16),
             pltpu.VMEM((3 * tok, rows), bf16),
-            pltpu.VMEM((heads, kv, tok), bf16),
             pltpu.VMEM((2, tok, tok), f32),
-            pltpu.VMEM((3, kv, tok), bf16),
-            pltpu.VMEM((kv, tok), f32),
-            pltpu.VMEM((3 * N_X - 1, quarter, tok), bf16),
+            pltpu.VMEM((2, tok, kv), bf16),
             pltpu.VMEM((2, kv, tok), bf16),
-            dma((4,)), dma, dma((2,)), dma((2,)),
-            dma((3 * N_X - 1,)), dma((3 * N_X - 1,)), dma((n_head - 1,)), dma((n_head - 1,)),
+            pltpu.VMEM((tok, kv), f32),
+            pltpu.VMEM((tok, kv), f32),
+            pltpu.VMEM((2 * N_X - 1, quarter, tok), bf16),
+            pltpu.VMEM((2, kv, tok), bf16),
+            dma((4,)), dma((2,)), dma((2,)), dma((2,)),
+            dma((2 * N_X - 1,)), dma((2 * N_X - 1,)), dma((n_head - 1,)), dma((n_head - 1,)),
             pltpu.SemaphoreType.REGULAR,
         ],
         compiler_params=pltpu.CompilerParams(
             collective_id=0, has_side_effects=True, vmem_limit_bytes=50 << 20),
         cost_estimate=pl.CostEstimate(flops=6 * 10**9, bytes_accessed=8 * 10**6, transcendentals=10**6),
         name="latent_backward",
-    )(q, kt, do, seg)
+    )(*[pltpu.with_memory_space_constraint(a, pltpu.HBM) for a in (q, kt, do, seg)])
+    dq, gc = pl.pallas_call(
+        store_kernel,
+        out_shape=(jax.ShapeDtypeStruct((heads, kv, tok), bf16), jax.ShapeDtypeStruct((kv, tok), bf16)),
+        in_specs=[pl.BlockSpec(memory_space=pltpu.VMEM)] * 2,
+        out_specs=(hbm, hbm),
+        scratch_shapes=[dma((2,))],
+        name="store",
+    )(*[pltpu.with_memory_space_constraint(a, pltpu.VMEM) for a in (dq, gc)])
     return jnp.transpose(dq, (2, 0, 1)), jnp.transpose(gc)
 
 

time: 42 us -> 34.6 us (0.82)
  local copies, waits for them, and re-layouts: 7.11 us -> 0 us
    unnamed x8 -> x0, local copies, waits for them, and re-layouts: 7.11 us -> none
    pallas_call x1 -> x2, Pallas kernels: 33.8 us -> 33.4 us  [the longest x1 31.9 us: local(): pl.pallas_call(functools.partial(kernel, n_seq, n_head), out_shape=(pltpu...]
where the time goes in v2:
time: 34.6 us; the launch traced here: 34 us
  Pallas kernels  33.4 us (97%)
  between operations  0.64 us (2%)
    pallas_call x1, Pallas kernels, local(): pl.pallas_call(functools.partial(kernel, n_seq, n_head), out_shape=(pltpu...  31.9 us
    pallas_call x1, Pallas kernels, local(): pl.pallas_call(store_kernel, out_shape=(jax.ShapeDtypeStruct((heads, kv,...  1.47 us

profile of v2, /device:TPU:8, one launch (start us, length us, event | category | flops | bytes accessed | tf_op | source)
XLA Modules:
  0.0 34.0 jit_solution(15147022088602880567)
XLA Ops:
  0.6 31.9 %latent_backward.1 = (bf16[16,576,128]{2,1,0:T(8,128)(2,1)S(1)}, bf16[576,128]{1,0:T(8,128)(2,1)S(1)}) custom-call(bf16[16,576,128]{2,1,0:T(8,128)(2,1)} %bitcast.6, bf16[576,128]{1,0:T(8,128)(2,1)} %bitcast.9, bf16[2048,512]{1,0:T(8,128)(2,1)} %bitcast.8, s32[32,128]{1,0:T(8,128)} %bitcast.11), custom_call_target="tpu_custom_call" | custom-call | flops 6000000000 | bytes 8000000 | tf_op jit(solution)/shard_map/latent_backward/pallas_call | solution.py:282
  32.6 1.5 %store.1 = (bf16[16,576,128]{2,1,0:T(8,128)(2,1)}, bf16[576,128]{1,0:T(8,128)(2,1)}) custom-call(bf16[16,576,128]{2,1,0:T(8,128)(2,1)S(1)} %get-tuple-element.6.dq, bf16[576,128]{1,0:T(8,128)(2,1)S(1)} %get-tuple-element.7.gc), custom_call_target="tpu_custom_call" | custom-call | tf_op jit(solution)/shard_map/store/pallas_call | solution.py:316

commit v3 on v2

--- a/solution.py
+++ b/solution.py
@@ -26,9 +26,9 @@
 
 
 def kernel(n_seq, n_head, q_hbm, kt_hbm, do_hbm, seg_hbm, dq, gc_ref,
-           q, kt, kk, do, doh, qn, dot_, seg, s0, g0, p_all, ds_all, mask,
-           pmid, psend, pown, pacc, rbuf, gbuf,
-           lsem, wsend, wrecv, msem, psems, precv, gsend, grecv, ready):
+           q, kt, kk, do, doh, qn, dot_, seg, s0, g0, sx, gx, p_all, ds_all, mask,
+           pmid, psend, pown, rbuf, gbuf,
+           lsem, wsend, wrecv, msem, psems, precv, gsend, grecv, here, ready):
     heads, kv, tok = q.shape
     pairs = heads // 2
     quarter = kv // N_X
@@ -45,34 +45,61 @@
     load_s.start()
 
     barrier = pltpu.get_barrier_semaphore()
-    for d in (1, 2):
-        @pl.when(s + d < n_seq)
-        def _():
-            pl.semaphore_signal(barrier, inc=1, device_id={"seq": s + d, "head": h}, device_id_type=MESH)
-
-        @pl.when(s - d >= 0)
-        def _():
-            pl.semaphore_signal(barrier, inc=1, device_id={"seq": s - d, "head": h}, device_id_type=MESH)
-    for d in range(1, n_head):
-        pl.semaphore_signal(barrier, inc=1, device_id={"seq": s, "head": (h + d) % n_head}, device_id_type=MESH)
-    ahead = jnp.minimum(n_seq - 1 - s, 2)
-    behind = jnp.minimum(s, 2)
-    pl.semaphore_wait(barrier, ahead + behind + n_head - 1)
-
-    win = [
-        pltpu.make_async_remote_copy(
-            src_ref=kt_hbm, dst_ref=kt.at[2 - d], send_sem=wsend.at[d - 1], recv_sem=wrecv.at[d - 1],
-            device_id={"seq": s + d, "head": h}, device_id_type=MESH)
-        for d in (1, 2)
-    ]
-    for d in (2, 1):
-        @pl.when(s + d < n_seq)
-        def _():
-            win[d - 1].start()
-
-        @pl.when(s - d < 0)
-        def _():
-            kt[2 - d] = jnp.zeros((kv, tok), bf16)
+    @pl.when(s + 2 < n_seq)
+    def _():
+        pl.semaphore_signal(barrier, inc=1, device_id={"seq": s + 2, "head": h}, device_id_type=MESH)
+
+    @pl.when(s >= 2)
+    def _():
+        pl.semaphore_signal(barrier, inc=1, device_id={"seq": s - 2, "head": h}, device_id_type=MESH)
+    pl.semaphore_signal(barrier, inc=1, device_id={"seq": s + 1 - 2 * core, "head": h}, device_id_type=MESH)
+
+    def tell_heads(sem):
+        for d in range(1, n_head):
+            pl.semaphore_signal(sem, inc=1, device_id={"seq": s, "head": (h + d) % n_head}, device_id_type=MESH)
+
+    @pl.when(h == 0)
+    def _():
+        tell_heads(barrier)
+    ends = (s < 2).astype(jnp.int32) + (s + 2 >= n_seq).astype(jnp.int32)
+    load_k.wait()
+    pl.semaphore_wait(barrier, 3 - ends + (h > 0).astype(jnp.int32))
+
+    half = kv // 2
+
+    def win_copy(slot, i):
+        part = pl.ds(i * half, half)
+        if slot == 0:
+            src, to = kt.at[2], s + 2
+        else:
+            src, to = kt.at[0], s + 1 - 2 * core
+        return pltpu.make_async_remote_copy(
+            src_ref=src.at[part], dst_ref=kt.at[slot, part], send_sem=wsend.at[2 * slot + i],
+            recv_sem=wrecv.at[2 * slot + i], device_id={"seq": to, "head": h}, device_id_type=MESH)
+
+    def own_copy(i):
+        part = pl.ds(i * half, half)
+        return pltpu.make_async_remote_copy(
+            src_ref=kt.at[2, part], dst_ref=kt.at[1, part], send_sem=wsend.at[2 + i],
+            recv_sem=wrecv.at[2 + i], device_id={"seq": s + 1, "head": h}, device_id_type=MESH)
+
+    @pl.when(s + 2 < n_seq)
+    def _():
+        for i in (0, 1):
+            win_copy(0, i).start()
+
+    @pl.when(core == 0)
+    def _():
+        for i in (0, 1):
+            own_copy(i).start()
+
+    @pl.when(s < 2)
+    def _():
+        kt[0] = jnp.zeros((kv, tok), bf16)
+
+    @pl.when(s == 0)
+    def _():
+        kt[1] = jnp.zeros((kv, tok), bf16)
 
     @pl.when(s + 2 >= n_seq)
     def _():
@@ -81,6 +108,10 @@
 
     load_do.start()
     load_q.start()
+
+    @pl.when(h > 0)
+    def _():
+        pl.semaphore_signal(here, inc=1, device_id={"seq": s, "head": 0}, device_id_type=MESH)
 
     load_s.wait()
     row = lax.broadcasted_iota(jnp.int32, (tok, tok), 0)
@@ -98,7 +129,6 @@
     mask[0] = jnp.where(seen_1, 0.0, masked_score)
     mask[1] = jnp.where(seen_p, 0.0, masked_score)
 
-    load_k.wait()
     kk[pl.ds(2 * tok, tok), :] = jnp.transpose(kt[2])
     load_do.wait()
     r = lax.broadcasted_iota(jnp.int32, (256, 256), 0)
@@ -120,50 +150,99 @@
         s0[:, lanes] = dot(kk[pl.ds(2 * tok, tok), :], pair(q, p))
         g0[:, lanes] = dot(kk[pl.ds(2 * tok, tok), :LATENT], pair(dot_, p))
 
+    @pl.when(h == 0)
+    def _():
+        pl.semaphore_wait(here, n_head - 1)
+        tell_heads(here)
+
     for hh in range(heads):
         qn[pl.ds(hh * tok, tok), :] = jnp.transpose(q[hh])
 
-    for d in (1, 2):
-        @pl.when(s - d >= 0)
-        def _():
-            win[d - 1].wait_recv()
-        kk[pl.ds((2 - d) * tok, tok), :] = jnp.transpose(kt[2 - d])
-    for d in range(1, N_X):
-        pl.semaphore_signal(ready, inc=1, device_id={"seq": s, "head": (h + 2 * d) % n_head}, device_id_type=MESH)
+    @pl.when(h > 0)
+    def _():
+        pl.semaphore_wait(here, 1)
 
     tri2 = jnp.concatenate([tri, tri], axis=1)
     m1 = jnp.concatenate([mask[0], mask[0]], axis=1)
     mp = jnp.concatenate([mask[1], mask[1]], axis=1)
-    for p in range(pairs):
-        lanes = pl.ds(p * 256, 256)
-        s12 = dot(kk[pl.ds(0, 2 * tok), :], pair(q, p))
-        g12 = dot(kk[pl.ds(0, 2 * tok), :LATENT], pair(dot_, p))
-        sp = jnp.where(tri2, s0[:, lanes], s12[:tok]) + mp
-        s1 = s12[tok:] + m1
+
+    def first(slot):
+        rows = pl.ds(slot * tok, tok)
+        kk[rows, :] = jnp.transpose(kt[slot])
+        for p in range(pairs):
+            lanes = pl.ds(p * 256, 256)
+            sx[:, lanes] = dot(kk[rows, :], pair(q, p))
+            gx[:, lanes] = dot(kk[rows, :LATENT], pair(dot_, p))
+
+    def second(slot):
+        rows = pl.ds(slot * tok, tok)
+        kk[rows, :] = jnp.transpose(kt[slot])
+        for p in range(pairs):
+            lanes = pl.ds(p * 256, 256)
+            sy = dot(kk[rows, :], pair(q, p))
+            gy = dot(kk[rows, :LATENT], pair(dot_, p))
+            s1, s2 = (sy, sx[:, lanes]) if slot == 1 else (sx[:, lanes], sy)
+            g1, g2 = (gy, gx[:, lanes]) if slot == 1 else (gx[:, lanes], gy)
+            weigh(lanes, s1, s2, g1, g2)
+
+    def weigh(lanes, s1, s2, g1, g2):
+        sp = jnp.where(tri2, s0[:, lanes], s2) + mp
+        s1 = s1 + m1
         top = jnp.maximum(jnp.max(sp, axis=0, keepdims=True), jnp.max(s1, axis=0, keepdims=True))
         ep = jnp.exp2((sp - top) * exp2_scale)
         e1 = jnp.exp2((s1 - top) * exp2_scale)
         inv = 1.0 / (jnp.sum(ep, axis=0, keepdims=True) + jnp.sum(e1, axis=0, keepdims=True))
         wp, w1 = ep * inv, e1 * inv
         wlp, wl1 = wp.astype(bf16), w1.astype(bf16)
-        gp, g1 = jnp.where(tri2, g0[:, lanes], g12[:tok]), g12[tok:]
+        gp = jnp.where(tri2, g0[:, lanes], g2)
         delta = (jnp.sum(wlp.astype(f32) * gp, axis=0, keepdims=True)
                  + jnp.sum(wl1.astype(f32) * g1, axis=0, keepdims=True))
         dsp = (score_scale * wp * (gp - delta)).astype(bf16)
         ds1 = (score_scale * w1 * (g1 - delta)).astype(bf16)
         zero = jnp.zeros_like(wlp)
-        p_all[0:tok, lanes] = jnp.where(tri2, zero, wlp)
-        p_all[tok:2 * tok, lanes] = wl1
+        p_all[tok:2 * tok, lanes] = jnp.where(tri2, zero, wlp)
+        p_all[0:tok, lanes] = wl1
         p_all[2 * tok:, lanes] = jnp.where(tri2, wlp, zero)
-        ds_all[0:tok, lanes] = jnp.where(tri2, zero, dsp)
-        ds_all[tok:2 * tok, lanes] = ds1
+        ds_all[tok:2 * tok, lanes] = jnp.where(tri2, zero, dsp)
+        ds_all[0:tok, lanes] = ds1
         ds_all[2 * tok:, lanes] = jnp.where(tri2, dsp, zero)
 
-    def key_grad(block):
-        rows = pl.ds(block * tok, tok)
-        pown[...] = dot(ds_all[rows, :], qn[...])
-        pown[:, :LATENT] += dot(p_all[rows, :], doh[...])
-        return pown[...]
+    def tell():
+        for d in range(1, N_X):
+            pl.semaphore_signal(ready, inc=1, device_id={"seq": s, "head": (h + 2 * d) % n_head}, device_id_type=MESH)
+
+    @pl.when(core == 0)
+    def _():
+        @pl.when(s >= 2)
+        def _():
+            for i in (0, 1):
+                win_copy(0, i).wait_recv()
+        tell()
+        first(0)
+
+        @pl.when(s >= 2)
+        def _():
+            for i in (0, 1):
+                win_copy(1, i).wait_recv()
+        second(1)
+
+    @pl.when(core == 1)
+    def _():
+        for i in (0, 1):
+            win_copy(1, i).wait_recv()
+        first(1)
+
+        @pl.when(s >= 2)
+        def _():
+            for i in (0, 1):
+                win_copy(0, i).wait_recv()
+                win_copy(1, i).start()
+        tell()
+        second(0)
+
+    def key_grad(rows):
+        from_keys = dot(ds_all[rows, :], qn[...])
+        return from_keys[:, :LATENT] + dot(p_all[rows, :], doh[...]), from_keys[:, LATENT:]
 
     swap = pltpu.make_async_remote_copy(
         src_ref=pmid.at[0], dst_ref=pmid.at[1], send_sem=msem.at[0], recv_sem=msem.at[1],
@@ -177,42 +256,48 @@
             dst_ref=rbuf.at[slot], send_sem=psems.at[slot], recv_sem=precv.at[slot],
             device_id={"seq": s - 2 * (1 - b), "head": xx * 2 + y}, device_id_type=MESH)
 
-    def middle():
-        pmid[0] = key_grad(1).astype(bf16)
-
-        @pl.when(s > 0)
-        def _():
-            swap.start()
+    low, high = key_grad(pl.ds(0, tok))
+    pmid[0, :, :LATENT] = low.astype(bf16)
+    pmid[0, :, LATENT:] = high.astype(bf16)
+
+    @pl.when(s > 0)
+    def _():
+        swap.start()
+    low, high = key_grad(pl.ds(tok, 2 * tok))
+    pown[:, :LATENT] = low
+    pown[:, LATENT:] = high
+    pl.semaphore_wait(ready, N_X - 1)
+
+    def emit(b, add):
+        rows = pl.ds(b * tok, tok)
+        if add:
+            swap.wait_recv()
+            psend[b] = jnp.transpose((pown[rows, :] + pmid[1].astype(f32)).astype(bf16))
+        else:
+            psend[b] = jnp.transpose(pown[rows, :].astype(bf16))
+        if b == 0:
+            @pl.when(s >= 2)
+            def _():
+                for j in (2, 1, 3, 0):
+                    part_copy(0, j).start()
+        else:
+            for j in (2, 1, 3):
+                part_copy(1, j).start()
 
     @pl.when(core == 0)
     def _():
-        pacc[...] = key_grad(2)
-        middle()
-        swap.wait_recv()
-        psend[1] = jnp.transpose((pacc[...] + pmid[1].astype(f32)).astype(bf16))
+        emit(0, False)
+        emit(1, True)
+
+    @pl.when((core == 1) & (s >= 2))
+    def _():
+        emit(0, True)
 
     @pl.when(core == 1)
     def _():
-        middle()
-        psend[1] = jnp.transpose(key_grad(2).astype(bf16))
-
-    pl.semaphore_wait(ready, N_X - 1)
-    for j in (2, 1, 3):
-        part_copy(1, j).start()
-
-    @pl.when(s >= 2)
-    def _():
-        key_grad(0)
-
-        @pl.when(core == 1)
-        def _():
-            swap.wait_recv()
-            pown[...] += pmid[1].astype(f32)
-        psend[0] = jnp.transpose(pown[...].astype(bf16))
-        for j in (2, 1, 3, 0):
-            part_copy(0, j).start()
-
-    ktall = jnp.concatenate([kt[0], kt[1], kt[2]], axis=1)
+        emit(1, False)
+
+    ktall = jnp.concatenate([kt[1], kt[0], kt[2]], axis=1)
     for p in range(pairs):
         out = dot(ktall, ds_all[:, pl.ds(p * 256, 256)]).astype(bf16)
         dq[2 * p] = out[:, :tok]
@@ -243,10 +328,16 @@
         gather_copy(d).wait_recv()
     gc_ref[...] = (gbuf[0].astype(f32) + gbuf[1].astype(f32)).astype(bf16)
 
-    for d in (1, 2):
-        @pl.when(s + d < n_seq)
-        def _():
-            win[d - 1].wait_send()
+    @pl.when(s + 2 < n_seq)
+    def _():
+        for i in (0, 1):
+            win_copy(0, i).wait_send()
+
+    @pl.when((core == 0) | (s >= 2))
+    def _():
+        for i in (0, 1):
+            win_copy(1, i).wait_send()
+
     @pl.when(s > 0)
     def _():
         swap.wait_send()
@@ -295,17 +386,19 @@
             pltpu.VMEM((n_seq, tok), jnp.int32),
             pltpu.VMEM((tok, rows), f32),
             pltpu.VMEM((tok, rows), f32),
+            pltpu.VMEM((tok, rows), f32),
+            pltpu.VMEM((tok, rows), f32),
             pltpu.VMEM((3 * tok, rows), bf16),
             pltpu.VMEM((3 * tok, rows), bf16),
             pltpu.VMEM((2, tok, tok), f32),
             pltpu.VMEM((2, tok, kv), bf16),
             pltpu.VMEM((2, kv, tok), bf16),
-            pltpu.VMEM((tok, kv), f32),
-            pltpu.VMEM((tok, kv), f32),
+            pltpu.VMEM((2 * tok, kv), f32),
             pltpu.VMEM((2 * N_X - 1, quarter, tok), bf16),
             pltpu.VMEM((2, kv, tok), bf16),
-            dma((4,)), dma((2,)), dma((2,)), dma((2,)),
+            dma((4,)), dma((4,)), dma((4,)), dma((2,)),
             dma((2 * N_X - 1,)), dma((2 * N_X - 1,)), dma((n_head - 1,)), dma((n_head - 1,)),
+            pltpu.SemaphoreType.REGULAR,
             pltpu.SemaphoreType.REGULAR,
         ],
         compiler_params=pltpu.CompilerParams(

time: 34.6 us -> 33 us (0.954); the launches traced: 34 us -> 32.9 us
  Pallas kernels: 33.4 us -> 32.3 us
    pallas_call x1, Pallas kernels: 31.9 us -> 30.8 us  [local(): pl.pallas_call(functools.partial(kernel, n_seq, n_head), out_shape=(pltpu...]
where the time goes in v3:
time: 33 us; the launch traced here: 32.9 us
  Pallas kernels  32.3 us (98%)
  between operations  0.64 us (2%)
    pallas_call x1, Pallas kernels, local(): pl.pallas_call(functools.partial(kernel, n_seq, n_head), out_shape=(pltpu...  30.8 us
    pallas_call x1, Pallas kernels, local(): pl.pallas_call(store_kernel, out_shape=(jax.ShapeDtypeStruct((heads, kv,...  1.47 us

profile of v3, /device:TPU:8, one launch (start us, length us, event | category | flops | bytes accessed | tf_op | source)
XLA Modules:
  0.0 32.9 jit_solution(7893951227469889941)
XLA Ops:
  0.6 30.8 %latent_backward.1 = (bf16[16,576,128]{2,1,0:T(8,128)(2,1)S(1)}, bf16[576,128]{1,0:T(8,128)(2,1)S(1)}) custom-call(bf16[16,576,128]{2,1,0:T(8,128)(2,1)} %bitcast.6, bf16[576,128]{1,0:T(8,128)(2,1)} %bitcast.9, bf16[2048,512]{1,0:T(8,128)(2,1)} %bitcast.8, s32[32,128]{1,0:T(8,128)} %bitcast.11), custom_call_target="tpu_custom_call" | custom-call | flops 6000000000 | bytes 8000000 | tf_op jit(solution)/shard_map/latent_backward/pallas_call | solution.py:373
  31.4 1.5 %store.1 = (bf16[16,576,128]{2,1,0:T(8,128)(2,1)}, bf16[576,128]{1,0:T(8,128)(2,1)}) custom-call(bf16[16,576,128]{2,1,0:T(8,128)(2,1)S(1)} %get-tuple-element.6.dq, bf16[576,128]{1,0:T(8,128)(2,1)S(1)} %get-tuple-element.7.gc), custom_call_target="tpu_custom_call" | custom-call | tf_op jit(solution)/shard_map/store/pallas_call | solution.py:409

commit v4 on v3

--- a/solution.py
+++ b/solution.py
@@ -248,12 +248,16 @@
         src_ref=pmid.at[0], dst_ref=pmid.at[1], send_sem=msem.at[0], recv_sem=msem.at[1],
         device_id={"seq": s + 1 - 2 * core, "head": h}, device_id_type=MESH)
 
-    def part_copy(b, j):
+    parts = ((0, 80), (80, quarter - 80))
+
+    def part_copy(b, j, i):
         xx = (x + j) % N_X
         slot = b * N_X + j - b
+        begin, size = parts[i]
         return pltpu.make_async_remote_copy(
-            src_ref=psend.at[b, pl.ds(pl.multiple_of(xx * quarter, 16), quarter)],
-            dst_ref=rbuf.at[slot], send_sem=psems.at[slot], recv_sem=precv.at[slot],
+            src_ref=psend.at[b, pl.ds(pl.multiple_of(xx * quarter + begin, 16), size)],
+            dst_ref=rbuf.at[slot, pl.ds(begin, size)], send_sem=psems.at[2 * slot + i],
+            recv_sem=precv.at[2 * slot + i],
             device_id={"seq": s - 2 * (1 - b), "head": xx * 2 + y}, device_id_type=MESH)
 
     low, high = key_grad(pl.ds(0, tok))
@@ -278,24 +282,26 @@
         if b == 0:
             @pl.when(s >= 2)
             def _():
-                for j in (2, 1, 3, 0):
-                    part_copy(0, j).start()
+                for i in (0, 1):
+                    for j in (2, 1, 3, 0):
+                        part_copy(0, j, i).start()
         else:
-            for j in (2, 1, 3):
-                part_copy(1, j).start()
+            for i in (0, 1):
+                for j in (2, 1, 3):
+                    part_copy(1, j, i).start()
 
     @pl.when(core == 0)
     def _():
+        emit(1, True)
         emit(0, False)
-        emit(1, True)
+
+    @pl.when(core == 1)
+    def _():
+        emit(1, False)
 
     @pl.when((core == 1) & (s >= 2))
     def _():
         emit(0, True)
-
-    @pl.when(core == 1)
-    def _():
-        emit(1, False)
 
     ktall = jnp.concatenate([kt[1], kt[0], kt[2]], axis=1)
     for p in range(pairs):
@@ -304,28 +310,34 @@
         dq[2 * p + 1] = out[:, tok:]
 
 
-    total = psend[1, pl.ds(pl.multiple_of(x * quarter, 16), quarter), :].astype(f32)
-    for j in range(1, N_X):
-        part_copy(1, j).wait_recv()
-        total = total + rbuf[N_X + j - 1].astype(f32)
-    for j in range(N_X):
+    def gather_copy(d, i):
+        begin, size = parts[i]
+        mine = pl.ds(pl.multiple_of(x * quarter + begin, 16), size)
+        return pltpu.make_async_remote_copy(
+            src_ref=gbuf.at[y, mine], dst_ref=gbuf.at[y, mine],
+            send_sem=gsend.at[2 * d - 2 + i], recv_sem=grecv.at[2 * d - 2 + i],
+            device_id={"seq": s, "head": (h + d) % n_head}, device_id_type=MESH)
+
+    for i in (0, 1):
+        begin, size = parts[i]
+        mine = pl.ds(pl.multiple_of(x * quarter + begin, 16), size)
+        total = psend[1, mine, :].astype(f32)
+        for j in range(1, N_X):
+            part_copy(1, j, i).wait_recv()
+            total = total + rbuf[N_X + j - 1, begin:begin + size].astype(f32)
+
         @pl.when(s + 2 < n_seq)
         def _():
-            part_copy(0, j).wait_recv()
-        total = total + rbuf[j].astype(f32)
-    mine = pl.ds(pl.multiple_of(x * quarter, 16), quarter)
-    gbuf[y, mine, :] = total.astype(bf16)
-
-    def gather_copy(d):
-        return pltpu.make_async_remote_copy(
-            src_ref=gbuf.at[y, mine], dst_ref=gbuf.at[y, mine],
-            send_sem=gsend.at[d - 1], recv_sem=grecv.at[d - 1],
-            device_id={"seq": s, "head": (h + d) % n_head}, device_id_type=MESH)
-
-    for d in (3, 5, 4, 1, 7, 2, 6):
-        gather_copy(d).start()
-    for d in (2, 6, 1, 7, 4, 3, 5):
-        gather_copy(d).wait_recv()
+            for j in range(N_X):
+                part_copy(0, j, i).wait_recv()
+        for j in range(N_X):
+            total = total + rbuf[j, begin:begin + size].astype(f32)
+        gbuf[y, mine, :] = total.astype(bf16)
+        for d in (3, 5, 4, 1, 7, 2, 6):
+            gather_copy(d, i).start()
+    for i in (0, 1):
+        for d in (2, 6, 1, 7, 4, 3, 5):
+            gather_copy(d, i).wait_recv()
     gc_ref[...] = (gbuf[0].astype(f32) + gbuf[1].astype(f32)).astype(bf16)
 
     @pl.when(s + 2 < n_seq)
@@ -345,11 +357,13 @@
     @pl.when(s >= 2)
     def _():
         for j in range(N_X):
-            part_copy(0, j).wait_send()
-    for j in range(1, N_X):
-        part_copy(1, j).wait_send()
-    for d in range(1, n_head):
-        gather_copy(d).wait_send()
+            for i in (0, 1):
+                part_copy(0, j, i).wait_send()
+    for i in (0, 1):
+        for j in range(1, N_X):
+            part_copy(1, j, i).wait_send()
+        for d in range(1, n_head):
+            gather_copy(d, i).wait_send()
 
 
 def store_kernel(dq, gc, dq_hbm, gc_hbm, sems):
@@ -397,7 +411,7 @@
             pltpu.VMEM((2 * N_X - 1, quarter, tok), bf16),
             pltpu.VMEM((2, kv, tok), bf16),
             dma((4,)), dma((4,)), dma((4,)), dma((2,)),
-            dma((2 * N_X - 1,)), dma((2 * N_X - 1,)), dma((n_head - 1,)), dma((n_head - 1,)),
+            dma((4 * N_X - 2,)), dma((4 * N_X - 2,)), dma((2 * n_head - 2,)), dma((2 * n_head - 2,)),
             pltpu.SemaphoreType.REGULAR,
             pltpu.SemaphoreType.REGULAR,
         ],

time: 33 us -> 32.1 us (0.973)
  Pallas kernels: 32.3 us -> 31.2 us
    pallas_call x1, Pallas kernels: 30.8 us -> 29.8 us  [local(): pl.pallas_call(functools.partial(kernel, n_seq, n_head), out_shape=(pltpu...]
where the time goes in v4:
time: 32.1 us; the launch traced here: 31.9 us
  Pallas kernels  31.2 us (97%)
  between operations  0.64 us (2%)
    pallas_call x1, Pallas kernels, local(): pl.pallas_call(functools.partial(kernel, n_seq, n_head), out_shape=(pltpu...  29.8 us
    pallas_call x1, Pallas kernels, local(): pl.pallas_call(store_kernel, out_shape=(jax.ShapeDtypeStruct((heads, kv,...  1.47 us

profile of v4, /device:TPU:8, one launch (start us, length us, event | category | flops | bytes accessed | tf_op | source)
XLA Modules:
  0.0 31.9 jit_solution(6119684529115022775)
XLA Ops:
  0.6 29.8 %latent_backward.1 = (bf16[16,576,128]{2,1,0:T(8,128)(2,1)S(1)}, bf16[576,128]{1,0:T(8,128)(2,1)S(1)}) custom-call(bf16[16,576,128]{2,1,0:T(8,128)(2,1)} %bitcast.6, bf16[576,128]{1,0:T(8,128)(2,1)} %bitcast.9, bf16[2048,512]{1,0:T(8,128)(2,1)} %bitcast.8, s32[32,128]{1,0:T(8,128)} %bitcast.11), custom_call_target="tpu_custom_call" | custom-call | flops 6000000000 | bytes 8000000 | tf_op jit(solution)/shard_map/latent_backward/pallas_call | solution.py:387
  30.4 1.5 %store.1 = (bf16[16,576,128]{2,1,0:T(8,128)(2,1)}, bf16[576,128]{1,0:T(8,128)(2,1)}) custom-call(bf16[16,576,128]{2,1,0:T(8,128)(2,1)S(1)} %get-tuple-element.6.dq, bf16[576,128]{1,0:T(8,128)(2,1)S(1)} %get-tuple-element.7.gc), custom_call_target="tpu_custom_call" | custom-call | tf_op jit(solution)/shard_map/store/pallas_call | solution.py:423
